TPU v7x, 256 devices: a whole 4x4x8 slice. The times are simulated.
256 devices in a mesh: expert: 64 (over y, z, core), etp: 4 (over x).
Axes of the slice: x: 4, y: 4, z: 8, core: 2. Of those that a mesh axis runs over, the one named last changes fastest.
Arguments:
- tokens: bfloat16 [8192, 1536], P('expert', 'etp'), may hold values from -6 to 6
- out_grad: bfloat16 [8192, 1536], P('expert', 'etp'), may hold values from -6 to 6
- expert_ids: int32 [8192, 4], P('expert'), may hold values from 0 to 63, as said below
- combine: bfloat16 [8192, 4], P('expert'), may hold values from 0.049804688 to 1
- w_gate: bfloat16 [64, 1536, 1536], P('expert', None, 'etp'), may hold values from -0.15625 to 0.15625
- w_up: bfloat16 [64, 1536, 1536], P('expert', None, 'etp'), may hold values from -0.15625 to 0.15625
- w_down: bfloat16 [64, 1536, 1536], P('expert', 'etp'), may hold values from -0.15625 to 0.15625
Outputs:
- grad_tokens: bfloat16 [8192, 1536], P('expert', 'etp')
- grad_combine: float32 [8192, 4], P('expert')
- grad_gate: float32 [64, 1536, 1536], P('expert', None, 'etp')
- grad_up: float32 [64, 1536, 1536], P('expert', None, 'etp')
- grad_down: float32 [64, 1536, 1536], P('expert', 'etp')
Inputs may be any that keep to these rules, and one draw needn't show every extreme that they name: `expert_ids`: each row names 4 different experts. In each aligned block of 128 rows no expert is named by more than 16 rows, and one expert, the same in every block, is named by exactly 16 rows of every block.
All inputs are finite; a program needn't handle non-finite values.
Results may differ from a plain program's by a relative error of at most 0.007.
Values may be sent and summed in bfloat16 or wider, within the bound.
A program may use at most 128 MiB of HBM per device.

v0:
```python
import jax
import jax.numpy as jnp
from jax import lax
from jax.sharding import PartitionSpec as P

ALPHA = 1.702


def expert_rows(rows_x, rows_dy, weight_c, gate_w, up_w, down_w):
    gate_pre = jnp.dot(rows_x, gate_w, preferred_element_type=jnp.float32)
    up_pre = jnp.dot(rows_x, up_w, preferred_element_type=jnp.float32)
    squash = jax.nn.sigmoid(ALPHA * gate_pre)
    glu_out = gate_pre * squash
    activation = (glu_out * (up_pre + 1.0)).astype(jnp.bfloat16)
    back_proj = lax.dot_general(
        rows_dy, down_w, (((1,), (1,)), ((), ())), preferred_element_type=jnp.float32
    )
    score_part = jnp.sum(activation.astype(jnp.float32) * back_proj, axis=1)
    weight_col = weight_c.astype(jnp.float32)[:, None]
    scaled_grad = (weight_col * rows_dy.astype(jnp.float32)).astype(jnp.bfloat16)
    act_grad = weight_col * back_proj
    slope = squash + ALPHA * gate_pre * squash * (1.0 - squash)
    gate_grad = (act_grad * (up_pre + 1.0) * slope).astype(jnp.bfloat16)
    up_grad = (act_grad * glu_out).astype(jnp.bfloat16)
    first_dims = (((0,), (0,)), ((), ()))
    down_total = lax.dot_general(
        activation, scaled_grad, first_dims, preferred_element_type=jnp.float32
    )
    gate_total = lax.dot_general(rows_x, gate_grad, first_dims, preferred_element_type=jnp.float32)
    up_total = lax.dot_general(rows_x, up_grad, first_dims, preferred_element_type=jnp.float32)
    last_dims = (((1,), (1,)), ((), ()))
    input_grad = lax.dot_general(gate_grad, gate_w, last_dims, preferred_element_type=jnp.float32)
    input_grad = input_grad + lax.dot_general(
        up_grad, up_w, last_dims, preferred_element_type=jnp.float32
    )
    return (input_grad, score_part, gate_total, up_total, down_total)


def with_zero_row(values):
    return jnp.concatenate([values, jnp.zeros((1, values.shape[1]), values.dtype)], axis=0)


def local(tokens, out_grad, expert_ids, combine, w_gate, w_up, w_down):
    expert_count = lax.axis_size("expert")
    tok_rows = tokens.shape[0]
    top_k = expert_ids.shape[1]
    slot_total = 2 * tok_rows * top_k
    capacity = slot_total // expert_count
    assigned = tok_rows * top_k
    flat_ids = expert_ids.reshape(-1)
    expert_hits = (flat_ids[:, None] == jnp.arange(expert_count, dtype=jnp.int32)[None, :]).astype(
        jnp.int32
    )
    ranks = jnp.sum((jnp.cumsum(expert_hits, axis=0) - 1) * expert_hits, axis=1)
    slot_of = flat_ids * capacity + ranks
    owner_row = (
        jnp.full((slot_total,), tok_rows, jnp.int32)
        .at[slot_of]
        .set(jnp.arange(assigned, dtype=jnp.int32) // top_k)
    )
    slot_weight = jnp.zeros((slot_total,), combine.dtype).at[slot_of].set(combine.reshape(-1))

    def slot_rows(values):
        return jnp.take(with_zero_row(values), owner_row, axis=0)

    full_x, full_dy = (
        lax.all_gather(tokens, "etp", axis=1, tiled=True),
        lax.all_gather(out_grad, "etp", axis=1, tiled=True),
    )
    slot_inputs, slot_cotangent, slot_scale = (
        lax.all_to_all(slot_rows(full_x), "expert", split_axis=0, concat_axis=0, tiled=True),
        lax.all_to_all(slot_rows(full_dy), "expert", split_axis=0, concat_axis=0, tiled=True),
        lax.all_to_all(slot_weight, "expert", split_axis=0, concat_axis=0, tiled=True),
    )
    input_grad, score_part, gate_total, up_total, down_total = expert_rows(
        slot_inputs, slot_cotangent, slot_scale, w_gate[0], w_up[0], w_down[0]
    )
    scores = lax.psum(score_part, "etp")
    back_rows, back_scores = (
        lax.all_to_all(input_grad, "expert", split_axis=0, concat_axis=0, tiled=True),
        lax.all_to_all(scores, "expert", split_axis=0, concat_axis=0, tiled=True),
    )
    per_token = (
        jnp.take(back_rows, slot_of, axis=0)
        .reshape(tok_rows, top_k, back_rows.shape[1])
        .sum(axis=1)
    )
    grad_tokens = lax.psum_scatter(per_token, "etp", scatter_dimension=1, tiled=True).astype(
        jnp.bfloat16
    )
    grad_combine = jnp.take(back_scores, slot_of, axis=0).reshape(tok_rows, top_k)
    return (grad_tokens, grad_combine, gate_total[None], up_total[None], down_total[None])


def solution(mesh):
    return jax.shard_map(
        local,
        mesh=mesh,
        in_specs=(
            P("expert", "etp"),
            P("expert", "etp"),
            P("expert", None),
            P("expert", None),
            P("expert", None, "etp"),
            P("expert", None, "etp"),
            P("expert", "etp", None),
        ),
        out_specs=(
            P("expert", "etp"),
            P("expert", None),
            P("expert", None, "etp"),
            P("expert", None, "etp"),
            P("expert", "etp", None),
        ),
        check_vma=False,
    )
```

profile of v0, /device:TPU:1, one launch (start us, length us, event | category | flops | bytes accessed | tf_op | source)
XLA Modules:
  0.0 470.3 jit_solution(18349691410976090063)
XLA Ops:
  7.2 0.9 copy.19
  9.4 1.2 reduce-window.6
  11.0 3.8 scatter_custom_fusion
  15.4 13.2 %all-to-all-start = ((bf16[64,16,1]{1,2,0:T(2,128)(2,1)}), bf16[64,16,1]{1,2,0:T(2,128)(2,1)S(1)}, u32[]{:S(2)}, u32[]{:S(2)}) async-start(bf16[64,16,1]{1,2,0:T(2,128)(2,1)} %all_to_all.52), calls=%async_computation | async-start | bytes 65536 | tf_op jit(solution)/shard_map/all_to_all | solution.py:73
  28.6 2.4 scatter_custom_fusion.1
  31.1 11.2 %all_gather.7 = bf16[128,1536]{1,0:T(8,128)(2,1)S(1)} all-gather(bf16[128,384]{1,0:T(8,128)(2,1)} %param.9), channel_id=1, replica_groups=mesh['expert'=64,'etp'=4] {'etp'}, dimensions={1}, use_global_device_ids=true | all-gather | bytes 491520 | tf_op jit(solution)/shard_map/all_gather | solution.py:67
  42.3 10.0 %all_gather.6 = bf16[128,1536]{1,0:T(8,128)(2,1)S(1)} all-gather(bf16[128,384]{1,0:T(8,128)(2,1)} %param.10), channel_id=1, replica_groups=mesh['expert'=64,'etp'=4] {'etp'}, dimensions={1}, use_global_device_ids=true | all-gather | bytes 491520 | tf_op jit(solution)/shard_map/all_gather | solution.py:68
  52.4 5.6 %gather_fusion.2 = bf16[1024,1536]{1,0:T(8,128)(2,1)} fusion(bf16[129,1536]{1,0:T(8,128)(2,1)S(1)} %concatenate.6, s32[1024]{0:T(1024)S(1)} %fusion.16), kind=kCustom, calls=%fused_computation.clone | custom fusion | bytes 6295552 | tf_op jit(solution)/shard_map/jit(_take)/gather | solution.py:64
  58.0 5.6 %gather_fusion.3 = bf16[1024,1536]{1,0:T(8,128)(2,1)} fusion(bf16[129,1536]{1,0:T(8,128)(2,1)S(1)} %concatenate.7, s32[1024]{0:T(1024)S(1)} %fusion.16), kind=kCustom, calls=%fused_computation.1.clone | custom fusion | bytes 6295552 | tf_op jit(solution)/shard_map/jit(_take)/gather | solution.py:64
  63.6 5.0 %broadcast_select_fusion.1 = (bf16[1024,1536]{1,0:T(8,128)(2,1)}, bf16[1024,1536]{1,0:T(8,128)(2,1)}) fusion(bf16[1024,1536]{1,0:T(8,128)(2,1)} %gather_fusion.2, pred[1024]{0:T(1024)(128)(4,1)S(1)} %compare_and_fusion.1, bf16[1024,1536]{1,0:T(8,128)(2,1)} %gather_fusion.3), kind=kLoop, calls=%fused_computation.12 | loop fusion | flops 3145728 | bytes 12583936 | tf_op jit(solution)/shard_map/jit(_take)/select_n | solution.py:64
  68.6 89.0 %all_to_all.58 = bf16[64,16,1536]{2,1,0:T(8,128)(2,1)} all-to-all(bf16[64,16,1536]{2,1,0:T(8,128)(2,1)} %bitcast.60), channel_id=1, replica_groups=mesh['expert'=64,'etp'=4] {'expert'}, dimensions={0} | all-to-all | bytes 6291456 | tf_op jit(solution)/shard_map/all_to_all | solution.py:71
  157.5 6.4 %all-to-all-start.1 = ((bf16[64,16,1536]{2,1,0:T(8,128)(2,1)}), bf16[64,16,1536]{2,1,0:T(8,128)(2,1)}, u32[]{:S(2)}, u32[]{:S(2)}) async-start(bf16[64,16,1536]{2,1,0:T(8,128)(2,1)} %bitcast.59), calls=%async_computation.1 | async-start | bytes 6291456 | tf_op jit(solution)/shard_map/all_to_all | solution.py:72
  164.1 4.6 fusion.6
  168.7 2.6 fusion.9
  171.3 66.0 %all-to-all-done.1 = bf16[64,16,1536]{2,1,0:T(8,128)(2,1)} async-done(((bf16[64,16,1536]{2,1,0:T(8,128)(2,1)}), bf16[64,16,1536]{2,1,0:T(8,128)(2,1)}, u32[]{:S(2)}, u32[]{:S(2)}) %all-to-all-start.1) | async-done | bytes 3145760 | tf_op jit(solution)/shard_map/all_to_all | solution.py:72
  237.3 6.5 %multiply_reduce_fusion = (f32[1024]{0:T(1024)S(1)}, bf16[1024,384]{0,1:T(8,128)(2,1)}, bf16[1024,384]{0,1:T(8,128)(2,1)S(1)}, bf16[1024,384]{0,1:T(8,128)(2,1)}) fusion(f32[1024,384]{0,1:T(8,128)} %fusion.9, f32[1024,384]{0,1:T(8,128)} %fusion.6, f32[1024]{0:T(1024)S(1)} %reshape.105, bf16[1024,1536]{1,0:T(8,128)(2,1)} %bitcast.4, ...), kind=kOutput, calls=%fused_computation.16 | convolution fusion | flops 1216216064 | bytes 9838592 | tf_op jit(solution)/shard_map/dot_general | solution.py:15
  243.9 14.0 %psum.7 = f32[64,16,1]{1,0,2:T(8,128)} all-reduce(f32[64,16,1]{1,0,2:T(8,128)S(1)} %all_to_all.49), channel_id=1, replica_groups=mesh['expert'=64,'etp'=4] {'etp'}, use_global_device_ids=true, to_apply=%region_8.10 | all-reduce | flops 1024 | bytes 8192 | tf_op jit(solution)/shard_map/psum | solution.py:78
  257.9 9.8 %all-to-all-start.4 = ((f32[64,16,1]{1,2,0:T(1,128)}), f32[64,16,1]{1,2,0:T(1,128)S(1)}, u32[]{:S(2)}, u32[]{:S(2)}) async-start(f32[64,16,1]{1,2,0:T(1,128)} %bitcast.12), calls=%async_computation.5 | async-start | bytes 65536 | tf_op jit(solution)/shard_map/all_to_all | solution.py:81
  267.7 1.9 fusion.4
  269.6 4.5 convolution_add_fusion
  274.1 2.8 all-to-all-done.4
  276.9 7.7 %all-to-all-start.3 = ((f32[64,16,1536]{2,1,0:T(8,128)}), f32[64,16,1536]{2,1,0:T(8,128)}, u32[]{:S(2)}, u32[]{:S(2)}) async-start(f32[64,16,1536]{2,1,0:T(8,128)} %bitcast.58), calls=%async_computation.3 | async-start | bytes 12582912 | tf_op jit(solution)/shard_map/all_to_all | solution.py:80
  286.3 2.3 gather_fusion.1
  288.8 136.7 %all-to-all-done.3 = f32[64,16,1536]{2,1,0:T(8,128)} async-done(((f32[64,16,1536]{2,1,0:T(8,128)}), f32[64,16,1536]{2,1,0:T(8,128)}, u32[]{:S(2)}, u32[]{:S(2)}) %all-to-all-start.3) | async-done | bytes 6291488 | tf_op jit(solution)/shard_map/all_to_all | solution.py:80
  425.5 7.4 %gather_fusion = f32[512,1536]{1,0:T(8,128)} fusion(f32[1024,1536]{1,0:T(8,128)} %bitcast.11, s32[1024]{0:T(1024)S(1)} %pad_clamp_fusion), kind=kCustom, calls=%fused_computation.2 | custom fusion | bytes 6293504 | tf_op jit(solution)/shard_map/jit(_take)/gather | solution.py:84
  432.9 4.8 %gather.16 = f32[128,4,1536]{2,1,0:T(4,128)} reshape(f32[512,1536]{1,0:T(8,128)} %gather_fusion) | data formatting | bytes 6291456 | tf_op jit(solution)/shard_map/jit(_take)/gather | solution.py:84
  437.7 5.2 %select_reduce_fusion = f32[128,1536]{1,0:T(8,128)} fusion(f32[128,4,1536]{2,1,0:T(4,128)} %gather.16, pred[128,4]{1,0:T(8,128)(4,1)S(1)} %get-tuple-element.17), kind=kLoop, calls=%fused_computation.10 | loop fusion | flops 1376256 | bytes 3932672 | tf_op jit(solution)/shard_map/reduce_sum | solution.py:86
  442.9 5.3 %convolution_bitcast_fusion.1 = f32[1,1536,384]{2,1,0:T(8,128)} fusion(bf16[1024,1536]{1,0:T(8,128)(2,1)} %bitcast.62, bf16[1024,384]{0,1:T(8,128)(2,1)S(1)} %get-tuple-element.20), kind=kOutput, calls=%fused_computation.15 | convolution fusion | flops 1207959552 | bytes 6291456 | tf_op jit(solution)/shard_map/dot_general | solution.py:29
  448.2 3.3 convolution_bitcast_fusion
  451.5 4.8 %fusion.2 = f32[1,384,1536]{2,1,0:T(8,128)} fusion(bf16[1024,384]{0,1:T(8,128)(2,1)S(1)} %copy-done.6, bf16[1024,1536]{1,0:T(8,128)(2,1)} %bitcast.4, f32[1024]{0:T(1024)S(1)} %reshape.105), kind=kOutput, calls=%fused_computation.13 | convolution fusion | flops 1212678144 | bytes 6295552 | tf_op jit(solution)/shard_map/dot_general | solution.py:26
  456.9 4.9 %reduce-scatter.2.cloned.1.call-done = f32[128,384]{1,0:T(8,128)} async-done(((f32[128,1536]{1,0:T(8,128)}), f32[128,384]{1,0:T(8,128)}) %reduce-scatter.2.cloned.1.call-update) | async-done | bytes 196624 | tf_op jit(solution)/shard_map/reduce_scatter | solution.py:88
  461.9 1.6 convert_element_type.41
  (46 shorter events, 5.2 us)
Async XLA Ops:
  7.2 156.9 %copy-start = (bf16[1,1536,384]{2,1,0:T(8,128)(2,1)S(1)}, bf16[1,1536,384]{2,1,0:T(8,128)(2,1)}, u32[]{:S(2)}) copy-start(bf16[1,1536,384]{2,1,0:T(8,128)(2,1)} %param.13) | copy-start | bytes 3538948
  15.4 53.1 %all-to-all-start = ((bf16[64,16,1]{1,2,0:T(2,128)(2,1)}), bf16[64,16,1]{1,2,0:T(2,128)(2,1)S(1)}, u32[]{:S(2)}, u32[]{:S(2)}) async-start(bf16[64,16,1]{1,2,0:T(2,128)(2,1)} %all_to_all.52), calls=%async_computation | async-start | bytes 65536 | tf_op jit(solution)/shard_map/all_to_all | solution.py:73
  157.5 79.8 %all-to-all-start.1 = ((bf16[64,16,1536]{2,1,0:T(8,128)(2,1)}), bf16[64,16,1536]{2,1,0:T(8,128)(2,1)}, u32[]{:S(2)}, u32[]{:S(2)}) async-start(bf16[64,16,1536]{2,1,0:T(8,128)(2,1)} %bitcast.59), calls=%async_computation.1 | async-start | bytes 6291456 | tf_op jit(solution)/shard_map/all_to_all | solution.py:72
  164.1 4.6 copy-start.1
  164.1 4.6 copy-start.3
  257.9 19.1 %all-to-all-start.4 = ((f32[64,16,1]{1,2,0:T(1,128)}), f32[64,16,1]{1,2,0:T(1,128)S(1)}, u32[]{:S(2)}, u32[]{:S(2)}) async-start(f32[64,16,1]{1,2,0:T(1,128)} %bitcast.12), calls=%async_computation.5 | async-start | bytes 65536 | tf_op jit(solution)/shard_map/all_to_all | solution.py:81
  267.7 1.9 copy-start.4
  276.9 148.5 %all-to-all-start.3 = ((f32[64,16,1536]{2,1,0:T(8,128)}), f32[64,16,1536]{2,1,0:T(8,128)}, u32[]{:S(2)}, u32[]{:S(2)}) async-start(f32[64,16,1536]{2,1,0:T(8,128)} %bitcast.58), calls=%async_computation.3 | async-start | bytes 12582912 | tf_op jit(solution)/shard_map/all_to_all | solution.py:80
  284.6 177.3 %reduce-scatter.2.cloned.1.call-start = ((), (), s32[]{:S(2)}) async-start(), calls=%async_computation.6 | async-start | bytes 983040 | tf_op jit(solution)/shard_map/reduce_scatter | solution.py:88
  442.9 5.3 %copy-start.2 = (bf16[64,16,1536]{2,1,0:T(8,128)(2,1)S(1)}, bf16[64,16,1536]{2,1,0:T(8,128)(2,1)}, u32[]{:S(2)}) copy-start(bf16[64,16,1536]{2,1,0:T(8,128)(2,1)} %all_to_all.58) | copy-start | bytes 9437188
  442.9 5.3 %copy-start.5 = (bf16[1024,384]{0,1:T(8,128)(2,1)S(1)}, bf16[1024,384]{0,1:T(8,128)(2,1)}, u32[]{:S(2)}) copy-start(bf16[1024,384]{0,1:T(8,128)(2,1)} %get-tuple-element.21) | copy-start | bytes 2359300
  448.2 3.3 copy-start.6
Sparse Core Ops, SparseCore 0:
  443.0 18.8 reduce-scatter.1
where the time goes:
time: 471 us; the launch traced here: 470 us
  waiting for transfers between devices  210 us (45%)
  blocking collectives  124 us (26%)
  starting transfers between devices  37.3 us (8%)
  local copies, waits for them, and re-layouts  36.6 us (8%)
  matrix products  33.4 us (7%)
  between operations  14.3 us (3%)
  other arithmetic  14.1 us (3%)
    all_to_all x1, waiting for transfers between devices, local(): lax.all_to_all(input_grad, 'expert', split_axis=0, concat_axis=0, tiled=T...  137 us
    all_to_all x1, blocking collectives, local(): lax.all_to_all(slot_rows(full_x), 'expert', split_axis=0, concat_axis=0,...  89 us
    all_to_all x1, waiting for transfers between devices, local(): lax.all_to_all(slot_rows(full_dy), 'expert', split_axis=0, concat_axis=0,...  66 us
    psum x1, blocking collectives, local(): scores = lax.psum(score_part, 'etp')  14 us
    all_to_all x1, starting transfers between devices, local(): lax.all_to_all(slot_weight, 'expert', split_axis=0, concat_axis=0, tiled=...  13.2 us
    gather x2, local copies, waits for them, and re-layouts, local(): jnp.take(back_rows, slot_of, axis=0)  12.2 us
    all_gather x1, blocking collectives, local(): lax.all_gather(tokens, 'etp', axis=1, tiled=True)  11.2 us
    gather x2, local copies, waits for them, and re-layouts, slot_rows(): return jnp.take(with_zero_row(values), owner_row, axis=0)  11.2 us
  transfers between devices with their start and end apart: 5, of which 4 were waited for; matrix products, arithmetic and copies ran while one was open for 11% of the time, Pallas kernels for 0%

commit v1 on v0

v1 whole, which is shorter than its diff:
```python
import functools

import jax
import jax.numpy as jnp
from jax import lax
from jax.experimental import pallas as pl
from jax.experimental.pallas import tpu as pltpu
from jax.sharding import PartitionSpec as P

ALPHA = 1.702
MESH = pl.DeviceIdType.MESH
NX, NY, NZ, NC = 4, 4, 8, 2
CAP = 16
TOP = 4
EARLY = 0
BF16, F32 = jnp.bfloat16, jnp.float32
NT = (((1,), (1,)), ((), ()))
TN = (((0,), (0,)), ((), ()))


def dot(a, b, dims=(((1,), (0,)), ((), ()))):
    return lax.dot_general(a, b, dims, preferred_element_type=F32)


def route_kernel(
    dims, tok_hbm, dy_hbm, meta_ref, wg_hbm, wu_hbm, wd_hbm,
    out_tok, out_score, out_x, out_sg, out_agu,
    zbuf, zmeta, ysend, yrecv, rows_x, rows_dy, wg, wu, wd, sg, agu,
    igb, rs1, rs2s, rs2, yrs, yrr, zrs, zrr, zss, zsr, xss, xsr, pmat,
    in_sem, w_sem, o_sem, e_send, e_recv, z_send, z_recv, zm_send, zm_recv, y_send, y_recv,
    x_send, x_recv, xf_send, xf_recv, r1_send, r1_recv, r2_send, r2_recv,
    yr_send, yr_recv, zr_send, zr_recv, zs_send, zs_recv, xs_send, xs_recv,
):
    tok, dl, ff, early = dims
    late = dl - early
    width = 2 * dl + 2 * (NX - 1) * early
    groups = NY * NC
    rows = groups * CAP
    e = lax.axis_index("expert")
    x = lax.axis_index("etp")
    y = e // (NZ * NC)
    z = lax.rem(e // NC, NZ)
    c = lax.rem(e, NC)
    q = y * NC + c
    xr = lax.rem(x + 1, NX)
    xl = lax.rem(x + NX - 1, NX)
    xo = lax.rem(x + 2, NX)

    def at(y_, z_, c_, x_):
        return ((y_ * NZ + z_) * NC + c_, x_)

    right, left = (e, xr), (e, xl)

    def remote(src, dst, send, recv, dev):
        return pltpu.make_async_remote_copy(
            src_ref=src, dst_ref=dst, send_sem=send, recv_sem=recv, device_id=dev, device_id_type=MESH
        )

    def lanes(start, size):
        return pl.ds(pl.multiple_of(start, 128), size)

    def group_rows(index):
        return pl.ds(pl.multiple_of(index * CAP, CAP), CAP)

    loads = [
        pltpu.make_async_copy(tok_hbm, zbuf.at[0, :, pl.ds(0, dl)], in_sem.at[0]),
        pltpu.make_async_copy(dy_hbm, zbuf.at[0, :, pl.ds(dl, dl)], in_sem.at[1]),
    ]
    weights = [
        pltpu.make_async_copy(wg_hbm, wg, w_sem.at[0]),
        pltpu.make_async_copy(wu_hbm, wu, w_sem.at[1]),
        pltpu.make_async_copy(wd_hbm, wd, w_sem.at[2]),
    ]
    for cp in loads + weights:
        cp.start()

    group_peers = [(dy, dc) for dy in range(NY) for dc in range(NC) if dy or dc]

    def group_peer(dy, dc):
        return lax.rem(y + dy, NY), lax.rem(c + dc, NC)

    barrier = pltpu.get_barrier_semaphore()
    peers = [at(group_peer(dy, dc)[0], z, group_peer(dy, dc)[1], x) for dy, dc in group_peers]
    peers += [(e, lax.rem(x + d, NX)) for d in range(1, NX)]
    peers += [at(y, lax.rem(z + d, NZ), c, x) for d in range(1, NZ)]
    for dev in peers:
        pl.semaphore_signal(barrier, inc=1, device_id=dev, device_id_type=MESH)

    experts = NY * NZ * NC
    ids = meta_ref[0:TOP, :]
    e_iota = lax.broadcasted_iota(jnp.int32, (experts, tok), 0).astype(F32)
    hits = [e_iota == ids[k : k + 1, :] for k in range(TOP)]
    named = functools.reduce(jnp.logical_or, hits)
    named = jnp.where(named, 1.0, 0.0).astype(BF16)
    before = lax.broadcasted_iota(jnp.int32, (tok, tok), 0) < lax.broadcasted_iota(jnp.int32, (tok, tok), 1)
    ranks = dot(named, jnp.where(before, 1.0, 0.0).astype(BF16))
    for k in range(TOP):
        rank = jnp.sum(jnp.where(hits[k], ranks, 0.0), axis=0, keepdims=True)
        zmeta[0, k : k + 1, :] = ids[k : k + 1, :] * CAP + rank
        zmeta[0, TOP + k : TOP + k + 1, :] = meta_ref[TOP + k : TOP + k + 1, :]

    for cp in loads:
        cp.wait()
    pl.semaphore_wait(barrier, len(peers))

    if early:
        copies = []
        for d in range(1, NX):
            base = 2 * dl + (NX - d - 1) * 2 * early
            for part in range(2):
                copies.append(remote(
                    zbuf.at[0, :, pl.ds(part * dl + late, early)],
                    zbuf.at[0, :, pl.ds(base + part * early, early)],
                    e_send.at[d - 1, part], e_recv.at[NX - d - 1, part], (e, lax.rem(x + d, NX)),
                ))
        for cp in copies:
            cp.start()
        for cp in copies:
            cp.wait()

    def z_copies(src, dst, dev):
        return (
            remote(zbuf.at[src], zbuf.at[dst], z_send.at[dst], z_recv.at[dst], dev),
            remote(zmeta.at[src], zmeta.at[dst], zm_send.at[dst], zm_recv.at[dst], dev),
        )

    z_up = at(y, lax.rem(z + 1, NZ), c, x)
    z_down = at(y, lax.rem(z + NZ - 1, NZ), c, x)
    for cp in z_copies(0, 1, z_up):
        cp.start()
    if NZ > 2:
        for cp in z_copies(0, 2, z_down):
            cp.start()

    def hit_masks(i):
        j = lax.broadcasted_iota(jnp.int32, (rows, tok), 0)
        expert = ((j // (CAP * NC)) * NZ + z) * NC + lax.rem(j // CAP, NC)
        code = (expert * CAP + lax.rem(j, CAP)).astype(F32)
        return [code == zmeta[i, k : k + 1, :] for k in range(TOP)]

    def stage_a(i):
        @pl.when(i > 0)
        def _():
            for cp in z_copies(0, i, z_up):
                cp.wait_recv()

        @pl.when((i > 0) & (i + 2 < NZ))
        def _():
            step = 2 * lax.rem(i, 2) - 1
            for cp in z_copies(i, i + 2, at(y, lax.rem(z + step + NZ, NZ), c, x)):
                cp.start()

        masks = hit_masks(i)
        pick = jnp.where(functools.reduce(jnp.logical_or, masks), 1.0, 0.0).astype(BF16)
        pmat[i] = pick
        scale = functools.reduce(
            jnp.add, [jnp.where(masks[k], zmeta[i, TOP + k : TOP + k + 1, :], 0.0) for k in range(TOP)]
        )
        scale = jnp.sum(scale, axis=1, keepdims=True)
        ysend[i, :, 0:width] = dot(pick, zbuf[i]).astype(BF16)
        ysend[i, :, width : width + 128] = jnp.broadcast_to(scale, (rows, 128)).astype(BF16)
        for dy, dc in group_peers:
            yp, cp_ = group_peer(dy, dc)
            remote(
                ysend.at[i, group_rows(yp * NC + cp_)], yrecv.at[i, group_rows(q)],
                y_send.at[i], y_recv.at[i], at(yp, z, cp_, x),
            ).start()
        yrecv[i, group_rows(q), :] = ysend[i, group_rows(q), :]

    others = pl.ds(0, rows - CAP)

    def chunk(i):
        return pl.ds(pl.multiple_of(i * rows, rows), rows)

    def x_copies(i):
        out = []
        for part, buf in enumerate((rows_x, rows_dy)):
            src = yrecv.at[i, :, pl.ds(part * dl, late)]
            dst = buf.at[chunk(i), lanes(x * dl, late)]
            out.append(remote(src, dst, x_send.at[i, part], x_recv.at[i, part], right))
            out.append(remote(src, dst, x_send.at[i, 2 + part], x_recv.at[i, 2 + part], left))
        return out

    def stage_b(i):
        remote(ysend.at[i, others], yrecv.at[i, others], y_send.at[i], y_recv.at[i], right).wait_recv()
        for cp in x_copies(i):
            cp.start()
        for part, buf in enumerate((rows_x, rows_dy)):
            buf[chunk(i), lanes(x * dl, dl)] = yrecv[i, :, part * dl : (part + 1) * dl]
            if early:
                for d in range(1, NX):
                    base = 2 * dl + (d - 1) * 2 * early + part * early
                    buf[chunk(i), lanes(lax.rem(x + d, NX) * dl + late, early)] = yrecv[i, :, base : base + early]

    def forward_copies(i):
        tok_ref = rows_x.at[chunk(i), lanes(xl * dl, late)]
        dy_ref = rows_dy.at[chunk(i), lanes(xr * dl, late)]
        return (
            remote(tok_ref, tok_ref, xf_send.at[i, 0], xf_recv.at[i, 0], right),
            remote(dy_ref, dy_ref, xf_send.at[i, 1], xf_recv.at[i, 1], left),
        )

    def stage_c(i):
        tr, tl, dr, dl_ = x_copies(i)
        fr, fl = forward_copies(i)
        tr.wait_recv()
        fr.start()
        dl_.wait_recv()
        fl.start()

    half = rows // 2
    halves = (pl.ds(0, half), pl.ds(half, half))

    def rs1_copies(i):
        return (
            remote(igb.at[i, halves[0], lanes(xo * dl, dl)], rs1.at[i, 0], r1_send.at[i, 0], r1_recv.at[i, 0], right),
            remote(igb.at[i, halves[1], lanes(xo * dl, dl)], rs1.at[i, 1], r1_send.at[i, 1], r1_recv.at[i, 1], left),
        )

    def stage_d(i):
        tr, tl, dr, dl_ = x_copies(i)
        tl.wait_recv()
        dr.wait_recv()
        for cp in forward_copies(i):
            cp.wait_recv()
        rx = rows_x[chunk(i), :]
        rdy = rows_dy[chunk(i), :]
        gate_pre = dot(rx, wg[...])
        up_one = dot(rx, wu[...]) + 1.0
        back = dot(rdy, wd[...], NT)
        scale = yrecv[i, :, width : width + 128].astype(F32)
        squash = jax.nn.sigmoid(ALPHA * gate_pre)
        glu = gate_pre * squash
        act = (glu * up_one).astype(BF16)
        score = jnp.sum(act.astype(F32) * back, axis=1, keepdims=True)
        score = jnp.broadcast_to(score, (rows, 128))
        top = score.astype(BF16)
        rest = (score - top.astype(F32)).astype(BF16)
        lane = lax.broadcasted_iota(jnp.int32, (rows, 128), 1)
        yrs[i, :, dl : dl + 128] = jnp.where(lane < 64, top.astype(F32), rest.astype(F32)).astype(BF16)
        act_grad = jnp.concatenate([scale] * (ff // 128), axis=1) * back
        slope = squash + ALPHA * gate_pre * squash * (1.0 - squash)
        gate_grad = (act_grad * up_one * slope).astype(BF16)
        up_grad = (act_grad * glu).astype(BF16)
        agu[chunk(i), 0:ff] = act
        agu[chunk(i), ff : 2 * ff] = gate_grad
        agu[chunk(i), 2 * ff : 3 * ff] = up_grad
        sg[chunk(i), :] = (
            jnp.concatenate([scale] * (NX * dl // 128), axis=1) * rdy.astype(F32)
        ).astype(BF16)
        igb[i] = (dot(gate_grad, wg[...], NT) + dot(up_grad, wu[...], NT)).astype(BF16)
        for cp in rs1_copies(i):
            cp.start()

    def rs2_copies(i):
        return (
            remote(rs2s.at[i, 0], rs2.at[i, 0], r2_send.at[i, 0], r2_recv.at[i, 0], right),
            remote(rs2s.at[i, 1], rs2.at[i, 1], r2_send.at[i, 1], r2_recv.at[i, 1], left),
        )

    def stage_e(i):
        first, second = rs1_copies(i)
        to_right, to_left = rs2_copies(i)
        first.wait_recv()
        rs2s[i, 0, halves[0], :] = (
            igb[i, halves[0], lanes(xr * dl, dl)].astype(F32) + rs1[i, 0].astype(F32)
        ).astype(BF16)
        rs2s[i, 0, halves[1], :] = igb[i, halves[1], lanes(xr * dl, dl)]
        to_right.start()
        second.wait_recv()
        rs2s[i, 1, halves[0], :] = igb[i, halves[0], lanes(xl * dl, dl)]
        rs2s[i, 1, halves[1], :] = (
            igb[i, halves[1], lanes(xl * dl, dl)].astype(F32) + rs1[i, 1].astype(F32)
        ).astype(BF16)
        to_left.start()

    def stage_f(i):
        for cp in rs2_copies(i):
            cp.wait_recv()
        total = igb[i, :, lanes(x * dl, dl)].astype(F32) + rs2[i, 0].astype(F32) + rs2[i, 1].astype(F32)
        yrs[i, :, 0:dl] = total.astype(BF16)
        for dy, dc in group_peers:
            yp, cp_ = group_peer(dy, dc)
            remote(
                yrs.at[i, group_rows(yp * NC + cp_)], yrr.at[i, group_rows(q)],
                yr_send.at[i], yr_recv.at[i], at(yp, z, cp_, x),
            ).start()
        yrr[i, group_rows(q), :] = yrs[i, group_rows(q), :]

    def z_back(i):
        step = (lax.rem(i, 2) * -2 + 1) * ((i + 1) // 2)
        dev = at(y, lax.rem(z + step + NZ, NZ), c, x)
        return (
            remote(zrs.at[i], zrr.at[i], zr_send.at[i], zr_recv.at[i], dev),
            remote(zss.at[i], zsr.at[i], zs_send.at[i], zs_recv.at[i], dev),
        )

    def stage_g(i):
        remote(yrs.at[i, others], yrr.at[i, others], yr_send.at[i], yr_recv.at[i], right).wait_recv()
        back = dot(pmat[i], yrr[i, :, 0:dl], TN)
        pair = yrr[i, :, dl : dl + 128].astype(F32)
        score = pair[:, 0:1] + pair[:, 64:65]
        masks = hit_masks(i)
        by_token = [jnp.sum(jnp.where(m, score, 0.0), axis=0, keepdims=True) for m in masks]
        by_token = jnp.concatenate(by_token + [jnp.zeros((8 - TOP, tok), F32)], axis=0)

        @pl.when(i == 0)
        def _():
            zrr[0] = back.astype(BF16)
            zsr[0] = by_token

        @pl.when(i > 0)
        def _():
            zrs[i] = back.astype(BF16)
            zss[i] = by_token
            for cp in z_back(i):
                cp.start()

    outs = [
        pltpu.make_async_copy(rows_x, out_x, o_sem.at[0]),
        pltpu.make_async_copy(sg, out_sg, o_sem.at[1]),
        pltpu.make_async_copy(agu, out_agu, o_sem.at[2]),
    ]

    stages = (stage_a, stage_b, stage_c, stage_d, stage_e, stage_f, stage_g)

    def step(t, carry):
        @pl.when(t == 3)
        def _():
            for cp in weights:
                cp.wait()

        for lag, stage in enumerate(stages):
            @pl.when((t >= lag) & (t < NZ + lag))
            def _():
                stage(t - lag)

            if lag == 3:
                @pl.when(t == NZ + 2)
                def _():
                    for cp in outs:
                        cp.start()
        return carry

    lax.fori_loop(0, NZ + len(stages) - 1, step, 0)

    def finish(i, carry):
        total, score = carry
        for cp in z_back(i):
            cp.wait_recv()
        return total + zrr[i].astype(F32), score + zsr[i]

    total, score = lax.fori_loop(1, NZ, finish, (zrr[0].astype(F32), zsr[0]))
    xss[...] = score
    shares = [
        remote(xss, xsr.at[NX - d - 1], xs_send.at[d - 1], xs_recv.at[NX - d - 1], (e, lax.rem(x + d, NX)))
        for d in range(1, NX)
    ]
    for cp in shares:
        cp.start()
    out_tok[...] = total.astype(BF16)

    def drain(i, carry):
        @pl.when(i > 0)
        def _():
            for cp in z_copies(0, i, z_up) + z_back(i):
                cp.wait_send()

        remote(ysend.at[i, others], yrecv.at[i, others], y_send.at[i], y_recv.at[i], right).wait_send()
        remote(yrs.at[i, others], yrr.at[i, others], yr_send.at[i], yr_recv.at[i], right).wait_send()
        for cp in tuple(x_copies(i)) + forward_copies(i) + rs1_copies(i) + rs2_copies(i):
            cp.wait_send()
        return carry

    lax.fori_loop(0, NZ, drain, 0)
    for cp in outs:
        cp.wait()
    for cp in shares:
        cp.wait()
    for d in range(1, NX):
        score = score + xsr[d - 1]
    out_score[...] = score


def route(tokens, out_grad, meta, w_gate, w_up, w_down):
    tok, dl = tokens.shape
    d, ff = w_gate.shape
    early = EARLY
    width = 2 * dl + 2 * (NX - 1) * early
    rows = NY * NC * CAP
    slots = NZ * rows
    any_spec = pl.BlockSpec(memory_space=pl.ANY)
    vmem = pl.BlockSpec(memory_space=pltpu.VMEM)
    sem = pltpu.SemaphoreType.DMA
    macs = 5 * slots * d * ff
    return pl.pallas_call(
        functools.partial(route_kernel, (tok, dl, ff, early)),
        out_shape=(
            jax.ShapeDtypeStruct((tok, dl), BF16),
            jax.ShapeDtypeStruct((8, tok), F32),
            jax.ShapeDtypeStruct((slots, d), BF16),
            jax.ShapeDtypeStruct((slots, d), BF16),
            jax.ShapeDtypeStruct((slots, 3 * ff), BF16),
        ),
        in_specs=[any_spec, any_spec, vmem, any_spec, any_spec, any_spec],
        out_specs=(vmem, vmem, any_spec, any_spec, any_spec),
        scratch_shapes=[
            pltpu.VMEM((NZ, tok, width), BF16),
            pltpu.VMEM((NZ, 8, tok), F32),
            pltpu.VMEM((NZ, rows, width + 128), BF16),
            pltpu.VMEM((NZ, rows, width + 128), BF16),
            pltpu.VMEM((slots, d), BF16),
            pltpu.VMEM((slots, d), BF16),
            pltpu.VMEM((d, ff), BF16),
            pltpu.VMEM((d, ff), BF16),
            pltpu.VMEM((ff, d), BF16),
            pltpu.VMEM((slots, d), BF16),
            pltpu.VMEM((slots, 3 * ff), BF16),
            pltpu.VMEM((NZ, rows, d), BF16),
            pltpu.VMEM((NZ, 2, rows // 2, dl), BF16),
            pltpu.VMEM((NZ, 2, rows, dl), BF16),
            pltpu.VMEM((NZ, 2, rows, dl), BF16),
            pltpu.VMEM((NZ, rows, dl + 128), BF16),
            pltpu.VMEM((NZ, rows, dl + 128), BF16),
            pltpu.VMEM((NZ, tok, dl), BF16),
            pltpu.VMEM((NZ, tok, dl), BF16),
            pltpu.VMEM((NZ, 8, tok), F32),
            pltpu.VMEM((NZ, 8, tok), F32),
            pltpu.VMEM((8, tok), F32),
            pltpu.VMEM((NX - 1, 8, tok), F32),
            pltpu.VMEM((NZ, rows, tok), BF16),
            sem((2,)), sem((3,)), sem((3,)),
            sem((NX - 1, 2)), sem((NX - 1, 2)),
            sem((NZ,)), sem((NZ,)), sem((NZ,)), sem((NZ,)),
            sem((NZ,)), sem((NZ,)),
            sem((NZ, 4)), sem((NZ, 4)), sem((NZ, 2)), sem((NZ, 2)),
            sem((NZ, 2)), sem((NZ, 2)), sem((NZ, 2)), sem((NZ, 2)),
            sem((NZ,)), sem((NZ,)), sem((NZ,)), sem((NZ,)), sem((NZ,)), sem((NZ,)),
            sem((NX - 1,)), sem((NX - 1,)),
        ],
        compiler_params=pltpu.CompilerParams(
            collective_id=0, has_side_effects=True, vmem_limit_bytes=56 * 2**20
        ),
        cost_estimate=pl.CostEstimate(flops=2 * macs, bytes_accessed=20 * 2**20, transcendentals=0),
        name="route",
    )(tokens, out_grad, meta, w_gate, w_up, w_down)


def weight_kernel(ff, x_ref, sg_ref, agu_ref, gate_ref, up_ref, down_ref):
    both = dot(x_ref[...], agu_ref[:, ff:], TN)
    gate_ref[0] = both[:, :ff]
    up_ref[0] = both[:, ff:]
    down_ref[0] = dot(agu_ref[:, :ff], sg_ref[...], TN)


def weight_grads(rows_x, sg, agu):
    slots, d = rows_x.shape
    ff = agu.shape[1] // 3
    tile = 256
    return pl.pallas_call(
        functools.partial(weight_kernel, ff),
        grid=(d // tile,),
        out_shape=(
            jax.ShapeDtypeStruct((1, d, ff), F32),
            jax.ShapeDtypeStruct((1, d, ff), F32),
            jax.ShapeDtypeStruct((1, ff, d), F32),
        ),
        in_specs=[
            pl.BlockSpec((slots, tile), lambda i: (0, i)),
            pl.BlockSpec((slots, tile), lambda i: (0, i)),
            pl.BlockSpec((slots, 3 * ff), lambda i: (0, 0)),
        ],
        out_specs=(
            pl.BlockSpec((1, tile, ff), lambda i: (0, i, 0)),
            pl.BlockSpec((1, tile, ff), lambda i: (0, i, 0)),
            pl.BlockSpec((1, ff, tile), lambda i: (0, 0, i)),
        ),
        compiler_params=pltpu.CompilerParams(vmem_limit_bytes=48 * 2**20),
        cost_estimate=pl.CostEstimate(
            flops=6 * slots * d * ff, bytes_accessed=16 * 2**20, transcendentals=0
        ),
        name="weight_grads",
    )(rows_x, sg, agu)


def local(tokens, out_grad, expert_ids, combine, w_gate, w_up, w_down):
    meta = jnp.concatenate([expert_ids.astype(F32).T, combine.astype(F32).T], axis=0)
    grad_tokens, score, rows_x, sg, agu = route(tokens, out_grad, meta, w_gate[0], w_up[0], w_down[0])
    gate_total, up_total, down_total = weight_grads(rows_x, sg, agu)
    return grad_tokens, score[:TOP].T, gate_total, up_total, down_total


def solution(mesh):
    return jax.shard_map(
        local,
        mesh=mesh,
        in_specs=(
            P("expert", "etp"),
            P("expert", "etp"),
            P("expert", None),
            P("expert", None),
            P("expert", None, "etp"),
            P("expert", None, "etp"),
            P("expert", "etp", None),
        ),
        out_specs=(
            P("expert", "etp"),
            P("expert", None),
            P("expert", None, "etp"),
            P("expert", None, "etp"),
            P("expert", "etp", None),
        ),
        check_vma=False,
    )
```

time: 471 us -> 138 us (0.29)
  waiting for transfers between devices: 210 us -> 0 us
  Pallas kernels: 0 us -> 129 us
  blocking collectives: 124 us -> 0 us
  starting transfers between devices: 37.3 us -> 0 us
  matrix products: 33.4 us -> 0 us
  local copies, waits for them, and re-layouts: 36.6 us -> 5.46 us
  between operations: 14.3 us -> 0.64 us
  other arithmetic: 14.1 us -> 1.97 us
    all_to_all x4 -> x0, waiting for transfers between devices: 206 us -> none  [the longest x1 137 us: local(): lax.all_to_all(input_grad, 'expert', split_axis=0, concat_axis=0, tiled=T...]
    pallas_call x0 -> x2, Pallas kernels: none -> 129 us  [the longest x1 121 us: route(): pl.pallas_call(functools.partial(route_kernel, (tok, dl, ff, early)), out...]
    all_to_all x1 -> x0, blocking collectives: 89 us -> none  [local(): lax.all_to_all(slot_rows(full_x), 'expert', split_axis=0, concat_axis=0,...]
    all_to_all x4 -> x0, starting transfers between devices: 37 us -> none  [the longest x1 13.2 us: local(): lax.all_to_all(slot_weight, 'expert', split_axis=0, concat_axis=0, tiled=...]
    dot_general x8 -> x0, matrix products: 33.4 us -> none  [the longest x1 6.47 us: expert_rows(): lax.dot_general(rows_dy, down_w, (((1,), (1,)), ((), ())), preferred_elem...]
    gather x6 -> x0, local copies, waits for them, and re-layouts: 25.8 us -> none  [the longest x2 12.2 us: local(): jnp.take(back_rows, slot_of, axis=0)]
    all_gather x2 -> x0, blocking collectives: 21.2 us -> none  [the longest x1 11.2 us: local(): lax.all_gather(tokens, 'etp', axis=1, tiled=True)]
    psum x1 -> x0, blocking collectives: 14 us -> none  [local(): scores = lax.psum(score_part, 'etp')]
  transfers between devices with their start and end apart: 5 -> 0, of which waited for: 4 -> 0; matrix products, arithmetic and copies ran while one was open for 11% -> 0% of each run, Pallas kernels for 0% -> 0%
where the time goes in v1:
time: 138 us
  Pallas kernels  129 us (93%)
  local copies, waits for them, and re-layouts  5.46 us (4%)
  other arithmetic  1.97 us (1%)
    pallas_call x1, Pallas kernels, route(): pl.pallas_call(functools.partial(route_kernel, (tok, dl, ff, early)), out...  121 us
    pallas_call x1, Pallas kernels, weight_grads(): pl.pallas_call(functools.partial(weight_kernel, ff), grid=(d // tile,), o...  8.02 us
    unnamed x7, local copies, waits for them, and re-layouts  4.2 us

profile of v1, /device:TPU:1, one launch (start us, length us, event | category | flops | bytes accessed | tf_op | source)
XLA Modules:
  0.0 137.5 jit_solution(7506148729327720779)
XLA Ops:
  0.6 0.7 convert_bitcast_fusion.1
  1.3 0.7 convert_bitcast_fusion
  2.0 0.6 pad_maximum_fusion.meta_ref
  2.6 121.5 %route.1 = (bf16[128,384]{1,0:T(8,128)(2,1)}, f32[8,128]{1,0:T(8,128)}, bf16[1024,1536]{1,0:T(8,128)(2,1)}, bf16[1024,1536]{1,0:T(8,128)(2,1)}, bf16[1024,1152]{1,0:T(8,128)(2,1)}) custom-call(bf16[128,384]{1,0:T(8,128)(2,1)} %tok_hbm.1, bf16[128,384]{1,0:T(8,128)(2,1)} %dy_hbm.1, f32[8,128]{1,0:T(8,128)} %pad_maximum_fusion.meta_ref, ...), custom_call_target="tpu_custom_call" | custom-call | flops 6039797760 | bytes 20971520 | tf_op jit(solution)/shard_map/route/pallas_call | solution.py:396
  124.1 1.3 slice_bitcast_fusion
  125.3 0.0 copy-start
  125.3 1.9 %copy-done = bf16[1024,1536]{1,0:T(8,128)(2,1)S(1)} copy-done((bf16[1024,1536]{1,0:T(8,128)(2,1)S(1)}, bf16[1024,1536]{1,0:T(8,128)(2,1)}, u32[]{:S(2)}) %copy-start) | copy-done | bytes 3145752
  127.2 0.0 copy-start.1
  127.2 1.7 %copy-done.1 = bf16[1024,1152]{1,0:T(8,128)(2,1)S(1)} copy-done((bf16[1024,1152]{1,0:T(8,128)(2,1)S(1)}, bf16[1024,1152]{1,0:T(8,128)(2,1)}, u32[]{:S(2)}) %copy-start.1) | copy-done | bytes 2359320
  128.9 0.0 copy-start.2
  128.9 8.0 %weight_grads.1 = (f32[1,1536,384]{2,1,0:T(8,128)}, f32[1,1536,384]{2,1,0:T(8,128)}, f32[1,384,1536]{2,1,0:T(8,128)}) custom-call(bf16[1024,1536]{1,0:T(8,128)(2,1)S(1)} %copy-done, bf16[1024,1536]{1,0:T(8,128)(2,1)} %get-tuple-element.16.sg_ref, bf16[1024,1152]{1,0:T(8,128)(2,1)S(1)} %copy-done.1), custom_call_target="tpu_custom_call" | custom-call | flops 3623878656 | bytes 16777216 | tf_op jit(solution)/shard_map/weight_grads/pallas_call | solution.py:460
  136.9 0.0 copy-done.2
  136.9 0.6 copy.13
Async XLA Ops:
  125.3 1.9 %copy-start = (bf16[1024,1536]{1,0:T(8,128)(2,1)S(1)}, bf16[1024,1536]{1,0:T(8,128)(2,1)}, u32[]{:S(2)}) copy-start(bf16[1024,1536]{1,0:T(8,128)(2,1)} %get-tuple-element.15.x_ref) | copy-start | bytes 9437188
  127.2 1.7 %copy-start.1 = (bf16[1024,1152]{1,0:T(8,128)(2,1)S(1)}, bf16[1024,1152]{1,0:T(8,128)(2,1)}, u32[]{:S(2)}) copy-start(bf16[1024,1152]{1,0:T(8,128)(2,1)} %get-tuple-element.17.agu_ref) | copy-start | bytes 7077892
  128.9 8.0 %copy-start.2 = (bf16[128,384]{1,0:T(8,128)(2,1)S(1)}, bf16[128,384]{1,0:T(8,128)(2,1)}, u32[]{:S(2)}) copy-start(bf16[128,384]{1,0:T(8,128)(2,1)} %get-tuple-element.26) | copy-start | bytes 294916

commit v2 on v1

v2 whole, which is shorter than its diff:
```python
import functools

import jax
import jax.numpy as jnp
from jax import lax
from jax.experimental import pallas as pl
from jax.experimental.pallas import tpu as pltpu
from jax.sharding import PartitionSpec as P

ALPHA = 1.702
MESH = pl.DeviceIdType.MESH
NX, NY, NZ, NC = 4, 4, 8, 2
CAP = 16
TOP = 4
EARLY = 128
BF16, F32 = jnp.bfloat16, jnp.float32
ORDER = (
    "A0H0B0A1C0A2B1H1",
    "B2A3C1D0H2B3E0H3",
    "A4C2D1C3A5B4E1A6",
    "H4D3B5A7F1C4D2B6",
    "H5C5F0D4H6B7G0C6",
    "D5E4H7G1C7D6E5F4",
    "E6D7F5E3G4F6E7G5",
    "F3G6E2W0F7G3F2G7",
    "W1W2W3G2W4W5",
)
NT = (((1,), (1,)), ((), ()))
TN = (((0,), (0,)), ((), ()))


def dot(a, b, dims=(((1,), (0,)), ((), ()))):
    return lax.dot_general(a, b, dims, preferred_element_type=F32)


def route_kernel(
    dims, tok_hbm, dy_hbm, ids_ref, combine_ref, wg_hbm, wu_hbm, wd_hbm,
    out_tok, out_score, gate_buf, up_buf, down_buf,
    zbuf, zmeta, ysend, yrecv, hsend, hrecv, rows_x, rows_dy, wgu, wd, sg, gu, x_t, act_t,
    igb, own, rs1, rs2, yrs, yrr, zrs, zrr, zss, zsr, sco, sci, pmat,
    in_sem, w_sem, e_send, e_recv, z_send, z_recv, zm_send, zm_recv, y_send, y_recv, h_send, h_recv,
    x_send, x_recv, xf_send, xf_recv, r1_send, r1_recv, r2_send, r2_recv,
    yr_send, yr_recv, zr_send, zr_recv, zs_send, zs_recv, sc_send, sc_recv,
):
    tok, dl, ff, early = dims
    late = dl - early
    width = 2 * dl + 2 * (NX - 1) * early
    groups = NY * NC
    rows = groups * CAP
    e = lax.axis_index("expert")
    x = lax.axis_index("etp")
    y = e // (NZ * NC)
    z = lax.rem(e // NC, NZ)
    c = lax.rem(e, NC)
    q = y * NC + c
    xr = lax.rem(x + 1, NX)
    xl = lax.rem(x + NX - 1, NX)
    xo = lax.rem(x + 2, NX)

    def at(y_, z_, c_, x_):
        return ((y_ * NZ + z_) * NC + c_, x_)

    right, left = (e, xr), (e, xl)

    def remote(src, dst, send, recv, dev):
        return pltpu.make_async_remote_copy(
            src_ref=src, dst_ref=dst, send_sem=send, recv_sem=recv, device_id=dev, device_id_type=MESH
        )

    def lanes(start, size):
        return pl.ds(pl.multiple_of(start, 128), size)

    def group_rows(index):
        return pl.ds(pl.multiple_of(index * CAP, CAP), CAP)

    loads = [
        pltpu.make_async_copy(tok_hbm, zbuf.at[0, :, pl.ds(0, dl)], in_sem.at[0]),
        pltpu.make_async_copy(dy_hbm, zbuf.at[0, :, pl.ds(dl, dl)], in_sem.at[1]),
    ]
    weights = [
        pltpu.make_async_copy(wg_hbm, wgu.at[:, pl.ds(0, ff)], w_sem.at[0]),
        pltpu.make_async_copy(wu_hbm, wgu.at[:, pl.ds(ff, ff)], w_sem.at[1]),
        pltpu.make_async_copy(wd_hbm, wd, w_sem.at[2]),
    ]
    for cp in loads:
        cp.start()

    group_peers = [(dy, dc) for dy in range(NY) for dc in range(NC) if dy or dc]

    def group_peer(dy, dc):
        return lax.rem(y + dy, NY), lax.rem(c + dc, NC)

    barrier = pltpu.get_barrier_semaphore()
    peers = [(e, lax.rem(x + d, NX)) for d in range(1, NX)]
    peers += [at(y, lax.rem(z + d, NZ), c, x) for d in range(1, NZ)]
    peers += [at(group_peer(dy, dc)[0], z, group_peer(dy, dc)[1], x) for dy, dc in group_peers]
    for dev in peers:
        pl.semaphore_signal(barrier, inc=1, device_id=dev, device_id_type=MESH)
    for cp in weights:
        cp.start()

    experts = NY * NZ * NC
    ids = ids_ref[...].astype(F32)
    e_iota = lax.broadcasted_iota(jnp.int32, (experts, tok), 0).astype(F32)
    hits = [e_iota == ids[k : k + 1, :] for k in range(TOP)]
    named = functools.reduce(jnp.logical_or, hits)
    named = jnp.where(named, 1.0, 0.0).astype(BF16)
    before = lax.broadcasted_iota(jnp.int32, (tok, tok), 0) < lax.broadcasted_iota(jnp.int32, (tok, tok), 1)
    ranks = dot(named, jnp.where(before, 1.0, 0.0).astype(BF16))
    for k in range(TOP):
        rank = jnp.sum(jnp.where(hits[k], ranks, 0.0), axis=0, keepdims=True)
        zmeta[0, k : k + 1, :] = ids[k : k + 1, :] * CAP + rank
    zmeta[0, TOP : 2 * TOP, :] = combine_ref[...].astype(F32)

    for cp in loads:
        cp.wait()
    pl.semaphore_wait(barrier, len(peers))

    early_copies = []
    for d in range(1, NX):
        base = 2 * dl + (NX - d - 1) * 2 * early
        for part in range(2):
            early_copies.append(remote(
                zbuf.at[0, :, pl.ds(part * dl + late, early)],
                zbuf.at[0, :, pl.ds(base + part * early, early)],
                e_send.at[d - 1, part], e_recv.at[NX - d - 1, part], (e, lax.rem(x + d, NX)),
            ))
    for cp in early_copies:
        cp.start()

    z_up = at(y, lax.rem(z + 1, NZ), c, x)
    z_down = at(y, lax.rem(z + NZ - 1, NZ), c, x)

    def z_own(src, dst, dev):
        part = pl.ds(0, 2 * dl)
        return (
            remote(zbuf.at[src, :, part], zbuf.at[dst, :, part], z_send.at[dst, 0], z_recv.at[dst, 0], dev),
            remote(zmeta.at[src], zmeta.at[dst], zm_send.at[dst], zm_recv.at[dst], dev),
        )

    def z_rest(src, dst, dev):
        part = pl.ds(2 * dl, width - 2 * dl)
        return (remote(zbuf.at[src, :, part], zbuf.at[dst, :, part], z_send.at[dst, 1], z_recv.at[dst, 1], dev),)

    for cp in z_own(0, 1, z_up) + z_own(0, 2, z_down):
        cp.start()

    def hit_masks(i):
        j = lax.broadcasted_iota(jnp.int32, (rows, tok), 0)
        expert = ((j // (CAP * NC)) * NZ + z) * NC + lax.rem(j // CAP, NC)
        code = (expert * CAP + lax.rem(j, CAP)).astype(F32)
        return [code == zmeta[i, k : k + 1, :] for k in range(TOP)]

    def to_groups(src, dst, send, recv):
        for dy, dc in group_peers:
            yp, cp_ = group_peer(dy, dc)
            remote(src.at[group_rows(yp * NC + cp_)], dst.at[group_rows(q)], send, recv, at(yp, z, cp_, x)).start()
        dst[group_rows(q), :] = src[group_rows(q), :]

    def from_groups(src, dst, send, recv):
        return remote(src.at[others], dst.at[others], send, recv, right)

    def onward(i):
        return at(y, lax.rem(z + 2 * lax.rem(i, 2) - 1 + NZ, NZ), c, x)

    def stage_a(i):
        @pl.when(i > 0)
        def _():
            for cp in z_own(0, i, z_up):
                cp.wait_recv()

        @pl.when((i > 0) & (i + 2 < NZ - 1))
        def _():
            for cp in z_own(i, i + 2, onward(i)):
                cp.start()

        @pl.when(i == NZ - 3)
        def _():
            for cp in z_own(i, NZ - 1, z_up):
                cp.start()

        masks = hit_masks(i)
        pick = jnp.where(functools.reduce(jnp.logical_or, masks), 1.0, 0.0).astype(BF16)
        pmat[i] = pick
        scale = functools.reduce(
            jnp.add, [jnp.where(masks[k], zmeta[i, TOP + k : TOP + k + 1, :], 0.0) for k in range(TOP)]
        )
        scale = jnp.sum(scale, axis=1, keepdims=True)
        ysend[i, :, 0 : 2 * dl] = dot(pick, zbuf[i, :, 0 : 2 * dl]).astype(BF16)
        ysend[i, :, 2 * dl : 2 * dl + 128] = jnp.broadcast_to(scale, (rows, 128)).astype(BF16)
        to_groups(ysend.at[i], yrecv.at[i], y_send.at[i], y_recv.at[i])

    def stage_h(i):
        @pl.when(i == 0)
        def _():
            for cp in early_copies:
                cp.wait()
            for cp in z_rest(0, 1, z_up) + z_rest(0, 2, z_down):
                cp.start()

        @pl.when(i > 0)
        def _():
            for cp in z_rest(0, i, z_up):
                cp.wait_recv()

        @pl.when((i > 0) & (i + 2 < NZ - 1))
        def _():
            for cp in z_rest(i, i + 2, onward(i)):
                cp.start()

        @pl.when(i == NZ - 2)
        def _():
            for cp in z_rest(i, NZ - 1, z_down):
                cp.start()

        hsend[i] = dot(pmat[i], zbuf[i, :, 2 * dl : width]).astype(BF16)
        to_groups(hsend.at[i], hrecv.at[i], h_send.at[i], h_recv.at[i])

    others = pl.ds(0, rows - CAP)

    def chunk(i):
        return pl.ds(pl.multiple_of(i * rows, rows), rows)

    def x_copies(i):
        out = []
        for part, buf in enumerate((rows_x, rows_dy)):
            src = yrecv.at[i, :, pl.ds(part * dl, late)]
            dst = buf.at[chunk(i), lanes(x * dl, late)]
            out.append(remote(src, dst, x_send.at[i, part], x_recv.at[i, part], right))
            out.append(remote(src, dst, x_send.at[i, 2 + part], x_recv.at[i, 2 + part], left))
        return out

    def stage_b(i):
        from_groups(ysend.at[i], yrecv.at[i], y_send.at[i], y_recv.at[i]).wait_recv()
        for cp in x_copies(i):
            cp.start()
        for part, buf in enumerate((rows_x, rows_dy)):
            buf[chunk(i), lanes(x * dl, dl)] = yrecv[i, :, part * dl : (part + 1) * dl]

    def forward_copies(i):
        tok_ref = rows_x.at[chunk(i), lanes(xl * dl, late)]
        dy_ref = rows_dy.at[chunk(i), lanes(xr * dl, late)]
        return (
            remote(tok_ref, tok_ref, xf_send.at[i, 0], xf_recv.at[i, 0], right),
            remote(dy_ref, dy_ref, xf_send.at[i, 1], xf_recv.at[i, 1], left),
        )

    def stage_c(i):
        tr, tl, dr, dl_ = x_copies(i)
        fr, fl = forward_copies(i)
        tr.wait_recv()
        fr.start()
        dl_.wait_recv()
        fl.start()

    half = rows // 2
    halves = (pl.ds(0, half), pl.ds(half, half))

    def rs1_copies(i):
        return (
            remote(igb.at[i, 2, halves[0]], rs1.at[i, 0], r1_send.at[i, 0], r1_recv.at[i, 0], right),
            remote(igb.at[i, 2, halves[1]], rs1.at[i, 1], r1_send.at[i, 1], r1_recv.at[i, 1], left),
        )

    def diagonal():
        row = lax.broadcasted_iota(jnp.int32, (rows, rows), 0)
        return row == lax.broadcasted_iota(jnp.int32, (rows, rows), 1)

    def score_copies(i):
        return [
            remote(
                sco.at[i], sci.at[i, NX - d - 1], sc_send.at[i, d - 1], sc_recv.at[i, NX - d - 1],
                (e, lax.rem(x + d, NX)),
            )
            for d in range(1, NX)
        ]

    def stage_d(i):
        tr, tl, dr, dl_ = x_copies(i)
        tl.wait_recv()
        dr.wait_recv()
        for cp in forward_copies(i):
            cp.wait_recv()
        from_groups(hsend.at[i], hrecv.at[i], h_send.at[i], h_recv.at[i]).wait_recv()
        for part, buf in enumerate((rows_x, rows_dy)):
            for d in range(1, NX):
                base = (d - 1) * 2 * early + part * early
                buf[chunk(i), lanes(lax.rem(x + d, NX) * dl + late, early)] = hrecv[i, :, base : base + early]
        rx = rows_x[chunk(i), :]
        rdy = rows_dy[chunk(i), :]
        both = dot(rx, wgu[...])
        gate_pre = both[:, 0:ff]
        up_one = both[:, ff:] + 1.0
        back = dot(rdy, wd[...], NT)
        scale = yrecv[i, :, 2 * dl : 2 * dl + 128].astype(F32)
        squash = jax.nn.sigmoid(ALPHA * gate_pre)
        glu = gate_pre * squash
        act = (glu * up_one).astype(BF16)
        act_grad = jnp.concatenate([scale] * (ff // 128), axis=1) * back
        slope = squash + ALPHA * gate_pre * squash * (1.0 - squash)
        gate_grad = (act_grad * up_one * slope).astype(BF16)
        up_grad = (act_grad * glu).astype(BF16)
        grads = jnp.concatenate([gate_grad, up_grad], axis=1)
        gu[chunk(i), :] = grads

        def piece(xd):
            return dot(grads, wgu[pl.ds(pl.multiple_of(xd * dl, 128), dl), :], NT)

        igb[i, 2] = piece(xo).astype(BF16)
        for cp in rs1_copies(i):
            cp.start()
        igb[i, 0] = piece(xr).astype(BF16)
        igb[i, 1] = piece(xl).astype(BF16)
        own[i] = piece(x)
        score = jnp.sum(act.astype(F32) * back, axis=1, keepdims=True)
        score = jnp.sum(jnp.where(diagonal(), score, 0.0), axis=0, keepdims=True)
        sco[i] = jnp.broadcast_to(score, (8, rows))
        for cp in score_copies(i):
            cp.start()
        sg[chunk(i), :] = (
            jnp.concatenate([scale] * (NX * dl // 128), axis=1) * rdy.astype(F32)
        ).astype(BF16)
        x_t[:, chunk(i)] = rx.T
        act_t[:, chunk(i)] = act.T

    def rs2_copies(i):
        return (
            remote(igb.at[i, 0], rs2.at[i, 0], r2_send.at[i, 0], r2_recv.at[i, 0], right),
            remote(igb.at[i, 1], rs2.at[i, 1], r2_send.at[i, 1], r2_recv.at[i, 1], left),
        )

    def stage_e(i):
        for side in range(2):
            rs1_copies(i)[side].wait_recv()
            igb[i, side, halves[side], :] = (
                igb[i, side, halves[side], :].astype(F32) + rs1[i, side].astype(F32)
            ).astype(BF16)
            rs2_copies(i)[side].start()

    def stage_f(i):
        for cp in rs2_copies(i):
            cp.wait_recv()
        total = own[i] + rs2[i, 0].astype(F32) + rs2[i, 1].astype(F32)
        yrs[i, :, 0:dl] = total.astype(BF16)
        for cp in score_copies(i):
            cp.wait_recv()
        score = (sco[i] + sci[i, 0] + sci[i, 1] + sci[i, 2])[0:1, :]
        score = jnp.sum(jnp.where(diagonal(), score, 0.0), axis=1, keepdims=True)
        score = jnp.broadcast_to(score, (rows, 128))
        top = score.astype(BF16).astype(F32)
        lane = lax.broadcasted_iota(jnp.int32, (rows, 128), 1)
        yrs[i, :, dl : dl + 128] = jnp.where(lane < 64, top, score - top).astype(BF16)
        to_groups(yrs.at[i], yrr.at[i], yr_send.at[i], yr_recv.at[i])

    def z_back(i):
        step = (lax.rem(i, 2) * -2 + 1) * ((i + 1) // 2)
        dev = at(y, lax.rem(z + step + NZ, NZ), c, x)
        return (
            remote(zrs.at[i], zrr.at[i], zr_send.at[i], zr_recv.at[i], dev),
            remote(zss.at[i], zsr.at[i], zs_send.at[i], zs_recv.at[i], dev),
        )

    def stage_g(i):
        from_groups(yrs.at[i], yrr.at[i], yr_send.at[i], yr_recv.at[i]).wait_recv()
        back = dot(pmat[i], yrr[i, :, 0:dl], TN)
        pair = yrr[i, :, dl : dl + 128].astype(F32)
        score = pair[:, 0:1] + pair[:, 64:65]
        masks = hit_masks(i)
        by_token = [jnp.sum(jnp.where(m, score, 0.0), axis=0, keepdims=True) for m in masks]
        by_token = jnp.concatenate(by_token + [jnp.zeros((8 - TOP, tok), F32)], axis=0)

        @pl.when(i == 0)
        def _():
            zrr[0] = back.astype(BF16)
            zsr[0] = by_token

        @pl.when(i > 0)
        def _():
            zrs[i] = back.astype(BF16)
            zss[i] = by_token
            for cp in z_back(i):
                cp.start()

    tile = 256
    def stage_w(n):
        part = pl.ds(pl.multiple_of(n * tile, tile), tile)
        both = dot(x_t[part, :], gu[...])
        gate_buf[part, :] = both[:, 0:ff]
        up_buf[part, :] = both[:, ff:]
        down_buf[:, part] = dot(act_t[...], sg[:, part])

    for cp in weights:
        cp.wait()

    stages = dict(
        A=stage_a, B=stage_b, C=stage_c, D=stage_d, E=stage_e, F=stage_f, G=stage_g, H=stage_h, W=stage_w
    )
    names = list(stages)
    joined = "".join(ORDER)
    steps = [joined[n : n + 2] for n in range(0, len(joined), 2)]
    codes = [names.index(p[0]) * 8 + int(p[1]) for p in steps]
    words = [sum(code << (7 * k) for k, code in enumerate(codes[n : n + 4])) for n in range(0, len(codes), 4)]

    def step(s, carry):
        word = jnp.int32(words[0])
        for n in range(1, len(words)):
            word = jnp.where(s // 4 == n, jnp.int32(words[n]), word)
        code = lax.shift_right_logical(word, 7 * lax.rem(s, 4)) & 127
        for n, name in enumerate(names):
            @pl.when(code // 8 == n)
            def _():
                stages[name](lax.rem(code, 8))
        return carry

    lax.fori_loop(0, len(steps), step, 0)

    def finish(i, carry):
        total, score = carry
        for cp in z_back(i):
            cp.wait_recv()
        return total + zrr[i].astype(F32), score + zsr[i]

    total, score = lax.fori_loop(1, NZ, finish, (zrr[0].astype(F32), zsr[0]))
    out_tok[...] = total.astype(BF16)
    out_score[...] = score[0:TOP, :]

    def drain(i, carry):
        @pl.when(i > 0)
        def _():
            for cp in z_own(0, i, z_up) + z_rest(0, i, z_up) + z_back(i):
                cp.wait_send()

        from_groups(ysend.at[i], yrecv.at[i], y_send.at[i], y_recv.at[i]).wait_send()
        from_groups(hsend.at[i], hrecv.at[i], h_send.at[i], h_recv.at[i]).wait_send()
        from_groups(yrs.at[i], yrr.at[i], yr_send.at[i], yr_recv.at[i]).wait_send()
        for cp in (*x_copies(i), *forward_copies(i), *rs1_copies(i), *rs2_copies(i), *score_copies(i)):
            cp.wait_send()
        return carry

    lax.fori_loop(0, NZ, drain, 0)


def route(tokens, out_grad, ids, combine, w_gate, w_up, w_down):
    tok, dl = tokens.shape
    d, ff = w_gate.shape
    early = EARLY
    width = 2 * dl + 2 * (NX - 1) * early
    rows = NY * NC * CAP
    slots = NZ * rows
    any_spec = pl.BlockSpec(memory_space=pl.ANY)
    vmem = pl.BlockSpec(memory_space=pltpu.VMEM)
    sem = pltpu.SemaphoreType.DMA
    return pl.pallas_call(
        functools.partial(route_kernel, (tok, dl, ff, early)),
        out_shape=(
            pltpu.VMEM((tok, dl), BF16),
            pltpu.VMEM((TOP, tok), F32),
            pltpu.VMEM((d, ff), F32),
            pltpu.VMEM((d, ff), F32),
            pltpu.VMEM((ff, d), F32),
        ),
        in_specs=[any_spec, any_spec, vmem, vmem, any_spec, any_spec, any_spec],
        out_specs=(vmem, vmem, vmem, vmem, vmem),
        scratch_shapes=[
            pltpu.VMEM((NZ, tok, width), BF16),
            pltpu.VMEM((NZ, 8, tok), F32),
            pltpu.VMEM((NZ, rows, 2 * dl + 128), BF16),
            pltpu.VMEM((NZ, rows, 2 * dl + 128), BF16),
            pltpu.VMEM((NZ, rows, width - 2 * dl), BF16),
            pltpu.VMEM((NZ, rows, width - 2 * dl), BF16),
            pltpu.VMEM((slots, d), BF16),
            pltpu.VMEM((slots, d), BF16),
            pltpu.VMEM((d, 2 * ff), BF16),
            pltpu.VMEM((ff, d), BF16),
            pltpu.VMEM((slots, d), BF16),
            pltpu.VMEM((slots, 2 * ff), BF16),
            pltpu.VMEM((d, slots), BF16),
            pltpu.VMEM((ff, slots), BF16),
            pltpu.VMEM((NZ, 3, rows, dl), BF16),
            pltpu.VMEM((NZ, rows, dl), F32),
            pltpu.VMEM((NZ, 2, rows // 2, dl), BF16),
            pltpu.VMEM((NZ, 2, rows, dl), BF16),
            pltpu.VMEM((NZ, rows, dl + 128), BF16),
            pltpu.VMEM((NZ, rows, dl + 128), BF16),
            pltpu.VMEM((NZ, tok, dl), BF16),
            pltpu.VMEM((NZ, tok, dl), BF16),
            pltpu.VMEM((NZ, 8, tok), F32),
            pltpu.VMEM((NZ, 8, tok), F32),
            pltpu.VMEM((NZ, 8, rows), F32),
            pltpu.VMEM((NZ, NX - 1, 8, rows), F32),
            pltpu.VMEM((NZ, rows, tok), BF16),
            sem((2,)), sem((3,)),
            sem((NX - 1, 2)), sem((NX - 1, 2)),
            sem((NZ, 2)), sem((NZ, 2)), sem((NZ,)), sem((NZ,)),
            sem((NZ,)), sem((NZ,)), sem((NZ,)), sem((NZ,)),
            sem((NZ, 4)), sem((NZ, 4)), sem((NZ, 2)), sem((NZ, 2)),
            sem((NZ, 2)), sem((NZ, 2)), sem((NZ, 2)), sem((NZ, 2)),
            sem((NZ,)), sem((NZ,)), sem((NZ,)), sem((NZ,)), sem((NZ,)), sem((NZ,)),
            sem((NZ, NX - 1)), sem((NZ, NX - 1)),
        ],
        compiler_params=pltpu.CompilerParams(
            collective_id=0, has_side_effects=True, vmem_limit_bytes=50 * 2**20
        ),
        cost_estimate=pl.CostEstimate(
            flops=16 * slots * d * ff, bytes_accessed=12 * 2**20, transcendentals=0
        ),
        name="route",
    )(tokens, out_grad, ids, combine, w_gate, w_up, w_down)


def place_kernel(pieces, *refs):
    count = len(pieces)
    srcs, dsts, sems = refs[:count], refs[count : 2 * count], refs[2 * count]
    copies = []
    for src, dst, n in zip(srcs, dsts, pieces):
        size = src.shape[0] // n
        for k in range(n):
            part = pl.ds(k * size, size)
            copies.append(pltpu.make_async_copy(src.at[part], dst.at[part], sems.at[len(copies)]))
    for cp in copies:
        cp.start()
    for cp in copies:
        cp.wait()


def place(*arrays):
    pieces = [2 if a.size > 2**17 else 1 for a in arrays]
    return pl.pallas_call(
        functools.partial(place_kernel, pieces),
        out_shape=[jax.ShapeDtypeStruct(a.shape, a.dtype) for a in arrays],
        in_specs=[pl.BlockSpec(memory_space=pltpu.VMEM)] * len(arrays),
        out_specs=[pl.BlockSpec(memory_space=pl.ANY)] * len(arrays),
        scratch_shapes=[pltpu.SemaphoreType.DMA((sum(pieces),))],
        compiler_params=pltpu.CompilerParams(vmem_limit_bytes=4 * 2**20),
        name="place",
    )(*arrays)


def local(tokens, out_grad, expert_ids, combine, w_gate, w_up, w_down):
    results = route(tokens, out_grad, expert_ids.T, combine.T, w_gate[0], w_up[0], w_down[0])
    grad_tokens, score, gate_total, up_total, down_total = place(*results)
    return grad_tokens, score.T, gate_total[None], up_total[None], down_total[None]


def solution(mesh):
    return jax.shard_map(
        local,
        mesh=mesh,
        in_specs=(
            P("expert", "etp"),
            P("expert", "etp"),
            P("expert", None),
            P("expert", None),
            P("expert", None, "etp"),
            P("expert", None, "etp"),
            P("expert", "etp", None),
        ),
        out_specs=(
            P("expert", "etp"),
            P("expert", None),
            P("expert", None, "etp"),
            P("expert", None, "etp"),
            P("expert", "etp", None),
        ),
        check_vma=False,
    )
```

time: 138 us -> 105 us (0.76)
  Pallas kernels: 129 us -> 104 us
  local copies, waits for them, and re-layouts: 5.46 us -> 0 us
  other arithmetic: 1.97 us -> 0 us
    pallas_call x1, Pallas kernels: 121 us -> 101 us  [route(): pl.pallas_call(functools.partial(route_kernel, (tok, dl, ff, early)), out...]
    pallas_call x1, Pallas kernels: 8.02 us -> 3.03 us  [place(): pl.pallas_call(functools.partial(place_kernel, pieces), out_shape=[jax.Sh...]
    unnamed x7 -> x0, local copies, waits for them, and re-layouts: 4.2 us -> none
where the time goes in v2:
time: 105 us
  Pallas kernels  104 us (99%)
    pallas_call x1, Pallas kernels, route(): pl.pallas_call(functools.partial(route_kernel, (tok, dl, ff, early)), out...  101 us
    pallas_call x1, Pallas kernels, place(): pl.pallas_call(functools.partial(place_kernel, pieces), out_shape=[jax.Sh...  3.03 us

profile of v2, /device:TPU:1, one launch (start us, length us, event | category | flops | bytes accessed | tf_op | source)
XLA Modules:
  0.0 104.9 jit_solution(10156404944410317941)
XLA Ops:
  0.6 101.2 %route.1 = (bf16[128,384]{1,0:T(8,128)(2,1)S(1)}, f32[4,128]{1,0:T(4,128)S(1)}, f32[1536,384]{1,0:T(8,128)S(1)}, f32[1536,384]{1,0:T(8,128)S(1)}, f32[384,1536]{1,0:T(8,128)S(1)}) custom-call(bf16[128,384]{1,0:T(8,128)(2,1)} %tok_hbm.1, bf16[128,384]{1,0:T(8,128)(2,1)} %dy_hbm.1, s32[4,128]{1,0:T(4,128)} %bitcast.15, bf16[4,128]{1,0:T(4,128)(2,1)} %bitcast.17, ...), custom_call_target="tpu_custom_call" | custom-call | flops 9663676416 | bytes 12582912 | tf_op jit(solution)/shard_map/route/pallas_call | solution.py:453
  101.9 3.0 %place.1 = (bf16[128,384]{1,0:T(8,128)(2,1)}, f32[4,128]{1,0:T(4,128)}, f32[1536,384]{1,0:T(8,128)}, f32[1536,384]{1,0:T(8,128)}, f32[384,1536]{1,0:T(8,128)}) custom-call(bf16[128,384]{1,0:T(8,128)(2,1)S(1)} %get-tuple-element.15.refs_0_, f32[4,128]{1,0:T(4,128)S(1)} %get-tuple-element.16.refs_1_, f32[1536,384]{1,0:T(8,128)S(1)} %get-tuple-element.17.refs_2_, ...), custom_call_target="tpu_custom_call" | custom-call | tf_op jit(solution)/shard_map/place/pallas_call | solution.py:528

commit v3 on v2

--- a/solution.py
+++ b/solution.py
@@ -14,16 +14,17 @@
 TOP = 4
 EARLY = 128
 BF16, F32 = jnp.bfloat16, jnp.float32
+LAST = 1
 ORDER = (
-    "A0H0B0A1C0A2B1H1",
-    "B2A3C1D0H2B3E0H3",
-    "A4C2D1C3A5B4E1A6",
-    "H4D3B5A7F1C4D2B6",
-    "H5C5F0D4H6B7G0C6",
-    "D5E4H7G1C7D6E5F4",
-    "E6D7F5E3G4F6E7G5",
-    "F3G6E2W0F7G3F2G7",
-    "W1W2W3G2W4W5",
+    "A1B0A2C0A3B1A4B2",
+    "H0B3A5C1C2B4A6H1",
+    "B5D0H2C3B6H3A7D1",
+    "H4C5C4H5D3C6B7H6",
+    "D2D5E3H7D6C7D4E6",
+    "F3D7E5W0F6E7G3F5",
+    "E2G6F7E4G5E1F2G7",
+    "F4E0F1G2W1G4F0G1",
+    "W2W3W4W5G0",
 )
 NT = (((1,), (1,)), ((), ()))
 TN = (((0,), (0,)), ((), ()))
@@ -112,8 +113,26 @@
         zmeta[0, k : k + 1, :] = ids[k : k + 1, :] * CAP + rank
     zmeta[0, TOP : 2 * TOP, :] = combine_ref[...].astype(F32)
 
+    def hit_masks(i):
+        j = lax.broadcasted_iota(jnp.int32, (rows, tok), 0)
+        expert = ((j // (CAP * NC)) * NZ + z) * NC + lax.rem(j // CAP, NC)
+        code = (expert * CAP + lax.rem(j, CAP)).astype(F32)
+        return [code == zmeta[i, k : k + 1, :] for k in range(TOP)]
+
+    def own_slots(i):
+        masks = hit_masks(i)
+        pick = jnp.where(functools.reduce(jnp.logical_or, masks), 1.0, 0.0).astype(BF16)
+        pmat[i] = pick
+        scale = functools.reduce(
+            jnp.add, [jnp.where(masks[k], zmeta[i, TOP + k : TOP + k + 1, :], 0.0) for k in range(TOP)]
+        )
+        scale = jnp.sum(scale, axis=1, keepdims=True)
+        ysend[i, :, 0 : 2 * dl] = dot(pick, zbuf[i, :, 0 : 2 * dl]).astype(BF16)
+        ysend[i, :, 2 * dl : 2 * dl + 128] = jnp.broadcast_to(scale, (rows, 128)).astype(BF16)
+
     for cp in loads:
         cp.wait()
+    own_slots(0)
     pl.semaphore_wait(barrier, len(peers))
 
     early_copies = []
@@ -125,9 +144,6 @@
                 zbuf.at[0, :, pl.ds(base + part * early, early)],
                 e_send.at[d - 1, part], e_recv.at[NX - d - 1, part], (e, lax.rem(x + d, NX)),
             ))
-    for cp in early_copies:
-        cp.start()
-
     z_up = at(y, lax.rem(z + 1, NZ), c, x)
     z_down = at(y, lax.rem(z + NZ - 1, NZ), c, x)
 
@@ -142,14 +158,6 @@
         part = pl.ds(2 * dl, width - 2 * dl)
         return (remote(zbuf.at[src, :, part], zbuf.at[dst, :, part], z_send.at[dst, 1], z_recv.at[dst, 1], dev),)
 
-    for cp in z_own(0, 1, z_up) + z_own(0, 2, z_down):
-        cp.start()
-
-    def hit_masks(i):
-        j = lax.broadcasted_iota(jnp.int32, (rows, tok), 0)
-        expert = ((j // (CAP * NC)) * NZ + z) * NC + lax.rem(j // CAP, NC)
-        code = (expert * CAP + lax.rem(j, CAP)).astype(F32)
-        return [code == zmeta[i, k : k + 1, :] for k in range(TOP)]
 
     def to_groups(src, dst, send, recv):
         for dy, dc in group_peers:
@@ -160,16 +168,20 @@
     def from_groups(src, dst, send, recv):
         return remote(src.at[others], dst.at[others], send, recv, right)
 
+    to_groups(ysend.at[0], yrecv.at[0], y_send.at[0], y_recv.at[0])
+    for cp in z_own(0, 1, z_up) + z_own(0, 2, z_down):
+        cp.start()
+    for cp in early_copies:
+        cp.start()
+
     def onward(i):
         return at(y, lax.rem(z + 2 * lax.rem(i, 2) - 1 + NZ, NZ), c, x)
 
     def stage_a(i):
-        @pl.when(i > 0)
-        def _():
-            for cp in z_own(0, i, z_up):
-                cp.wait_recv()
-
-        @pl.when((i > 0) & (i + 2 < NZ - 1))
+        for cp in z_own(0, i, z_up):
+            cp.wait_recv()
+
+        @pl.when(i + 2 < NZ - 1)
         def _():
             for cp in z_own(i, i + 2, onward(i)):
                 cp.start()
@@ -179,15 +191,7 @@
             for cp in z_own(i, NZ - 1, z_up):
                 cp.start()
 
-        masks = hit_masks(i)
-        pick = jnp.where(functools.reduce(jnp.logical_or, masks), 1.0, 0.0).astype(BF16)
-        pmat[i] = pick
-        scale = functools.reduce(
-            jnp.add, [jnp.where(masks[k], zmeta[i, TOP + k : TOP + k + 1, :], 0.0) for k in range(TOP)]
-        )
-        scale = jnp.sum(scale, axis=1, keepdims=True)
-        ysend[i, :, 0 : 2 * dl] = dot(pick, zbuf[i, :, 0 : 2 * dl]).astype(BF16)
-        ysend[i, :, 2 * dl : 2 * dl + 128] = jnp.broadcast_to(scale, (rows, 128)).astype(BF16)
+        own_slots(i)
         to_groups(ysend.at[i], yrecv.at[i], y_send.at[i], y_recv.at[i])
 
     def stage_h(i):
@@ -381,6 +385,17 @@
             for cp in z_back(i):
                 cp.start()
 
+        @pl.when(i > 0)
+        def _():
+            for cp in z_own(0, i, z_up) + z_rest(0, i, z_up):
+                cp.wait_send()
+
+        from_groups(ysend.at[i], yrecv.at[i], y_send.at[i], y_recv.at[i]).wait_send()
+        from_groups(hsend.at[i], hrecv.at[i], h_send.at[i], h_recv.at[i]).wait_send()
+        from_groups(yrs.at[i], yrr.at[i], yr_send.at[i], yr_recv.at[i]).wait_send()
+        for cp in (*x_copies(i), *forward_copies(i), *rs1_copies(i), *rs2_copies(i), *score_copies(i)):
+            cp.wait_send()
+
     tile = 256
     def stage_w(n):
         part = pl.ds(pl.multiple_of(n * tile, tile), tile)
@@ -414,30 +429,16 @@
 
     lax.fori_loop(0, len(steps), step, 0)
 
-    def finish(i, carry):
+    def finish(p, carry):
+        i = jnp.where(p == NZ - 1, LAST, jnp.where(p < LAST, p, p + 1))
         total, score = carry
         for cp in z_back(i):
-            cp.wait_recv()
+            cp.wait()
         return total + zrr[i].astype(F32), score + zsr[i]
 
     total, score = lax.fori_loop(1, NZ, finish, (zrr[0].astype(F32), zsr[0]))
     out_tok[...] = total.astype(BF16)
     out_score[...] = score[0:TOP, :]
-
-    def drain(i, carry):
-        @pl.when(i > 0)
-        def _():
-            for cp in z_own(0, i, z_up) + z_rest(0, i, z_up) + z_back(i):
-                cp.wait_send()
-
-        from_groups(ysend.at[i], yrecv.at[i], y_send.at[i], y_recv.at[i]).wait_send()
-        from_groups(hsend.at[i], hrecv.at[i], h_send.at[i], h_recv.at[i]).wait_send()
-        from_groups(yrs.at[i], yrr.at[i], yr_send.at[i], yr_recv.at[i]).wait_send()
-        for cp in (*x_copies(i), *forward_copies(i), *rs1_copies(i), *rs2_copies(i), *score_copies(i)):
-            cp.wait_send()
-        return carry
-
-    lax.fori_loop(0, NZ, drain, 0)
 
 
 def route(tokens, out_grad, ids, combine, w_gate, w_up, w_down):

time: 105 us -> 99.1 us (0.944)
  Pallas kernels: 104 us -> 97.3 us
    pallas_call x1, Pallas kernels: 101 us -> 94.3 us  [route(): pl.pallas_call(functools.partial(route_kernel, (tok, dl, ff, early)), out...]
where the time goes in v3:
time: 99.1 us; the launch traced here: 98 us
  Pallas kernels  97.3 us (98%)
    pallas_call x1, Pallas kernels, route(): pl.pallas_call(functools.partial(route_kernel, (tok, dl, ff, early)), out...  94.3 us
    pallas_call x1, Pallas kernels, place(): pl.pallas_call(functools.partial(place_kernel, pieces), out_shape=[jax.Sh...  3.03 us

profile of v3, /device:TPU:1, one launch (start us, length us, event | category | flops | bytes accessed | tf_op | source)
XLA Modules:
  0.0 98.0 jit_solution(856170945649152110)
XLA Ops:
  0.6 94.3 %route.1 = (bf16[128,384]{1,0:T(8,128)(2,1)S(1)}, f32[4,128]{1,0:T(4,128)S(1)}, f32[1536,384]{1,0:T(8,128)S(1)}, f32[1536,384]{1,0:T(8,128)S(1)}, f32[384,1536]{1,0:T(8,128)S(1)}) custom-call(bf16[128,384]{1,0:T(8,128)(2,1)} %tok_hbm.1, bf16[128,384]{1,0:T(8,128)(2,1)} %dy_hbm.1, s32[4,128]{1,0:T(4,128)} %bitcast.15, bf16[4,128]{1,0:T(4,128)(2,1)} %bitcast.17, ...), custom_call_target="tpu_custom_call" | custom-call | flops 9663676416 | bytes 12582912 | tf_op jit(solution)/shard_map/route/pallas_call | solution.py:454
  94.9 3.0 %place.1 = (bf16[128,384]{1,0:T(8,128)(2,1)}, f32[4,128]{1,0:T(4,128)}, f32[1536,384]{1,0:T(8,128)}, f32[1536,384]{1,0:T(8,128)}, f32[384,1536]{1,0:T(8,128)}) custom-call(bf16[128,384]{1,0:T(8,128)(2,1)S(1)} %get-tuple-element.15.refs_0_, f32[4,128]{1,0:T(4,128)S(1)} %get-tuple-element.16.refs_1_, f32[1536,384]{1,0:T(8,128)S(1)} %get-tuple-element.17.refs_2_, ...), custom_call_target="tpu_custom_call" | custom-call | tf_op jit(solution)/shard_map/place/pallas_call | solution.py:529

commit v4 on v3

--- a/solution.py
+++ b/solution.py
@@ -14,17 +14,17 @@
 TOP = 4
 EARLY = 128
 BF16, F32 = jnp.bfloat16, jnp.float32
-LAST = 1
+LAST = 2
 ORDER = (
-    "A1B0A2C0A3B1A4B2",
-    "H0B3A5C1C2B4A6H1",
-    "B5D0H2C3B6H3A7D1",
-    "H4C5C4H5D3C6B7H6",
-    "D2D5E3H7D6C7D4E6",
-    "F3D7E5W0F6E7G3F5",
-    "E2G6F7E4G5E1F2G7",
-    "F4E0F1G2W1G4F0G1",
-    "W2W3W4W5G0",
+    "B0A1A2C0A3B1B2A4",
+    "H0B3A5C1H1B4C2A6",
+    "B5H2C3D1C4B6H3H4",
+    "E1C5A7H5C6D4B7H6",
+    "D5E4D6F1C7H7E5F4",
+    "D3E6G1D7G4F5E3D2",
+    "F6E7G5D0G6F3E2W0",
+    "F7W1E0W2G3F2G7W3",
+    "F0W4W5G2G0",
 )
 NT = (((1,), (1,)), ((), ()))
 TN = (((0,), (0,)), ((), ()))
@@ -93,7 +93,7 @@
 
     barrier = pltpu.get_barrier_semaphore()
     peers = [(e, lax.rem(x + d, NX)) for d in range(1, NX)]
-    peers += [at(y, lax.rem(z + d, NZ), c, x) for d in range(1, NZ)]
+    peers += [at(y, lax.rem(z + d, NZ), c, x) for d in (1, NZ - 1)]
     peers += [at(group_peer(dy, dc)[0], z, group_peer(dy, dc)[1], x) for dy, dc in group_peers]
     for dev in peers:
         pl.semaphore_signal(barrier, inc=1, device_id=dev, device_id_type=MESH)

time: 99.1 us -> 97.9 us (0.988); the launches traced: 98 us -> 97.8 us
  no operation moved by 1% of the time
where the time goes in v4:
time: 97.9 us; the launch traced here: 97.8 us
  Pallas kernels  97.2 us (99%)
    pallas_call x1, Pallas kernels, route(): pl.pallas_call(functools.partial(route_kernel, (tok, dl, ff, early)), out...  94.1 us
    pallas_call x1, Pallas kernels, place(): pl.pallas_call(functools.partial(place_kernel, pieces), out_shape=[jax.Sh...  3.03 us

profile of v4, /device:TPU:1, one launch (start us, length us, event | category | flops | bytes accessed | tf_op | source)
XLA Modules:
  0.0 97.8 jit_solution(17457323598480652666)
XLA Ops:
  0.6 94.1 %route.1 = (bf16[128,384]{1,0:T(8,128)(2,1)S(1)}, f32[4,128]{1,0:T(4,128)S(1)}, f32[1536,384]{1,0:T(8,128)S(1)}, f32[1536,384]{1,0:T(8,128)S(1)}, f32[384,1536]{1,0:T(8,128)S(1)}) custom-call(bf16[128,384]{1,0:T(8,128)(2,1)} %tok_hbm.1, bf16[128,384]{1,0:T(8,128)(2,1)} %dy_hbm.1, s32[4,128]{1,0:T(4,128)} %bitcast.15, bf16[4,128]{1,0:T(4,128)(2,1)} %bitcast.17, ...), custom_call_target="tpu_custom_call" | custom-call | flops 9663676416 | bytes 12582912 | tf_op jit(solution)/shard_map/route/pallas_call | solution.py:454
  94.8 3.0 %place.1 = (bf16[128,384]{1,0:T(8,128)(2,1)}, f32[4,128]{1,0:T(4,128)}, f32[1536,384]{1,0:T(8,128)}, f32[1536,384]{1,0:T(8,128)}, f32[384,1536]{1,0:T(8,128)}) custom-call(bf16[128,384]{1,0:T(8,128)(2,1)S(1)} %get-tuple-element.15.refs_0_, f32[4,128]{1,0:T(4,128)S(1)} %get-tuple-element.16.refs_1_, f32[1536,384]{1,0:T(8,128)S(1)} %get-tuple-element.17.refs_2_, ...), custom_call_target="tpu_custom_call" | custom-call | tf_op jit(solution)/shard_map/place/pallas_call | solution.py:529

commit v5 on v4

--- a/solution.py
+++ b/solution.py
@@ -236,7 +236,8 @@
 
     def stage_b(i):
         from_groups(ysend.at[i], yrecv.at[i], y_send.at[i], y_recv.at[i]).wait_recv()
-        for cp in x_copies(i):
+        to_right, to_left, dy_right, dy_left = x_copies(i)
+        for cp in (to_right, dy_left, to_left, dy_right):
             cp.start()
         for part, buf in enumerate((rows_x, rows_dy)):
             buf[chunk(i), lanes(x * dl, dl)] = yrecv[i, :, part * dl : (part + 1) * dl]

time: 97.9 us -> 97.5 us (level)
  no operation moved by 1% of the time
where the time goes in v5:
time: 97.5 us; the launch traced here: 97.4 us
  Pallas kernels  96.7 us (99%)
    pallas_call x1, Pallas kernels, route(): pl.pallas_call(functools.partial(route_kernel, (tok, dl, ff, early)), out...  93.7 us
    pallas_call x1, Pallas kernels, place(): pl.pallas_call(functools.partial(place_kernel, pieces), out_shape=[jax.Sh...  3.03 us

profile of v5, /device:TPU:1, one launch (start us, length us, event | category | flops | bytes accessed | tf_op | source)
XLA Modules:
  0.0 97.4 jit_solution(1530721651656771168)
XLA Ops:
  0.6 93.7 %route.1 = (bf16[128,384]{1,0:T(8,128)(2,1)S(1)}, f32[4,128]{1,0:T(4,128)S(1)}, f32[1536,384]{1,0:T(8,128)S(1)}, f32[1536,384]{1,0:T(8,128)S(1)}, f32[384,1536]{1,0:T(8,128)S(1)}) custom-call(bf16[128,384]{1,0:T(8,128)(2,1)} %tok_hbm.1, bf16[128,384]{1,0:T(8,128)(2,1)} %dy_hbm.1, s32[4,128]{1,0:T(4,128)} %bitcast.15, bf16[4,128]{1,0:T(4,128)(2,1)} %bitcast.17, ...), custom_call_target="tpu_custom_call" | custom-call | flops 9663676416 | bytes 12582912 | tf_op jit(solution)/shard_map/route/pallas_call | solution.py:455
  94.3 3.0 %place.1 = (bf16[128,384]{1,0:T(8,128)(2,1)}, f32[4,128]{1,0:T(4,128)}, f32[1536,384]{1,0:T(8,128)}, f32[1536,384]{1,0:T(8,128)}, f32[384,1536]{1,0:T(8,128)}) custom-call(bf16[128,384]{1,0:T(8,128)(2,1)S(1)} %get-tuple-element.15.refs_0_, f32[4,128]{1,0:T(4,128)S(1)} %get-tuple-element.16.refs_1_, f32[1536,384]{1,0:T(8,128)S(1)} %get-tuple-element.17.refs_2_, ...), custom_call_target="tpu_custom_call" | custom-call | tf_op jit(solution)/shard_map/place/pallas_call | solution.py:530
